TPU v7x, 128 devices: a whole 4x4x4 slice. The times are simulated.
128 devices in a mesh: dp: 8 (over z, core), tensor: 16 (over y, x).
Axes of the slice: x: 4, y: 4, z: 4, core: 2. Of those that a mesh axis runs over, the one named last changes fastest.
Arguments:
- activations: bfloat16 [65536, 4096], P(('dp', 'tensor')), may hold values from -6 to 6
- cotangent: bfloat16 [65536, 11008], P('dp', 'tensor'), may hold values from -0.008178711 to 0.008178711
- projection: bfloat16 [4096, 512], replicated, may hold values from -0.25 to 0.25
- first_moment: float32 [512, 11008], P('dp', 'tensor'), may hold values from -0.6 to 0.6
- second_moment: float32 [512, 11008], P('dp', 'tensor'), may hold values from 0.01 to 1
- step_count: int32 [1], replicated, may hold values from 1 to 39
Outputs:
- update: bfloat16 [4096, 11008], P('dp', 'tensor')
- new_first: float32 [512, 11008], P('dp', 'tensor')
- new_second: float32 [512, 11008], P('dp', 'tensor')
All inputs are finite; a program needn't handle non-finite values.
Results may differ from a plain program's by a relative error of at most 0.0055.
Values may be sent and summed in bfloat16 or wider, within the bound.
A program may use at most 128 MiB of HBM per device.

v0:
```python
import jax
import jax.numpy as jnp
from jax import lax
from jax.sharding import PartitionSpec as P


def in_blocks(shard, dim, count):
    before, after = (shard.shape[:dim], shard.shape[dim + 1 :])
    return jnp.moveaxis(shard.reshape(*before, count, -1, *after), dim, 0)


def sum_at_owner(shard, axis, dim):
    count = lax.axis_size(axis)
    parts = lax.all_to_all(in_blocks(shard, dim, count), axis, 0, 0, tiled=True)
    return jnp.sum(parts, axis=0)


def laid_out(parts, dim):
    parts = jnp.moveaxis(parts, 0, dim)
    shape = parts.shape
    return parts.reshape(*shape[:dim], shape[dim] * shape[dim + 1], *shape[dim + 2 :])


def sent_to_all(shard, axis):
    count = lax.axis_size(axis)
    return lax.all_to_all(
        jnp.broadcast_to(shard[None], (count, *shard.shape)), axis, 0, 0, tiled=True
    )


def gather_directly(shard, axis, dim):
    return laid_out(sent_to_all(shard, axis), dim)


def per_device(activations, cotangent, projection, first_moment, second_moment, step_count):
    projected = jnp.dot(activations, projection, preferred_element_type=jnp.float32).astype(
        jnp.bfloat16
    )
    width = projection.shape[0]
    replica = lax.axis_index("dp")
    partial_grad = lax.dot_general(
        lax.all_gather(projected, "tensor", axis=0, tiled=True),
        cotangent,
        (((0,), (0,)), ((), ())),
        preferred_element_type=jnp.float32,
    )
    grad = sum_at_owner(partial_grad, "dp", 0)
    t_value = step_count[0].astype(jnp.float32)
    new_first = 0.9 * first_moment + 0.1 * grad
    new_second = 0.999 * second_moment + 0.001 * grad * grad
    first_hat = new_first / (1.0 - jnp.power(jnp.float32(0.9), t_value))
    second_hat = new_second / (1.0 - jnp.power(jnp.float32(0.999), t_value))
    normalized = (first_hat / (jnp.sqrt(second_hat) + 1e-08)).astype(jnp.bfloat16)
    whole_steps = gather_directly(normalized, "dp", 0)
    out_rows = width // lax.axis_size("dp")
    local_projection = lax.dynamic_slice_in_dim(projection, replica * out_rows, out_rows, 0)
    update = jnp.dot(local_projection, whole_steps, preferred_element_type=jnp.float32).astype(
        jnp.bfloat16
    )
    return (update, new_first, new_second)


def solution(mesh):
    in_specs = (
        P(("dp", "tensor"), None),
        P("dp", "tensor"),
        P(),
        P("dp", "tensor"),
        P("dp", "tensor"),
        P(),
    )
    out_specs = (P("dp", "tensor"), P("dp", "tensor"), P("dp", "tensor"))
    return jax.shard_map(
        per_device, mesh=mesh, in_specs=in_specs, out_specs=out_specs, check_vma=False
    )
```

profile of v0, /device:TPU:1, one launch (start us, length us, event | category | flops | bytes accessed | tf_op | source)
XLA Modules:
  0.0 154.9 jit_solution(16666026992883483268)
XLA Ops:
  7.2 0.0 all-gather.2.cloned.1.call-start
  7.2 6.6 %convolution_convert_fusion.1 = bf16[512,512]{1,0:T(8,128)(2,1)} fusion(bf16[512,4096]{1,0:T(8,128)(2,1)} %param.6, bf16[4096,512]{1,0:T(8,128)(2,1)} %param.8), kind=kOutput, calls=%fused_computation.1 | convolution fusion | flops 2147745792 | bytes 8912896 | tf_op jit(solution)/shard_map/dot_general | solution.py:36
  13.8 0.0 all-gather.2.cloned.1.call-update
  13.8 74.0 %all-gather.2.cloned.1.call-done = bf16[8192,512]{1,0:T(8,128)(2,1)} async-done(((bf16[512,512]{1,0:T(8,128)(2,1)}), bf16[8192,512]{1,0:T(8,128)(2,1)}) %all-gather.2.cloned.1.call-update) | async-done | bytes 8388624 | tf_op jit(solution)/shard_map/all_gather | solution.py:42
  87.8 13.3 %fusion.4 = f32[512,688]{1,0:T(8,128)} fusion(bf16[8192,512]{1,0:T(8,128)(2,1)} %all-gather.2.cloned.1.call-done, bf16[8192,688]{0,1:T(8,128)(2,1)} %param.7), kind=kOutput, calls=%fused_computation.8 | convolution fusion | flops 5771362304 | bytes 21069824 | tf_op jit(solution)/shard_map/dot_general | solution.py:41
  101.1 0.0 copy-start
  101.1 0.0 copy-start.1
  101.1 5.2 %all-to-all-start = ((f32[8,64,688]{2,1,0:T(8,128)}), f32[8,64,688]{2,1,0:T(8,128)S(1)}, u32[]{:S(2)}, u32[]{:S(2)}) async-start(f32[8,64,688]{2,1,0:T(8,128)} %bitcast), calls=%async_computation | async-start | bytes 3145728 | tf_op jit(solution)/shard_map/all_to_all | solution.py:14
  107.1 20.0 %all-to-all-done = f32[8,64,688]{2,1,0:T(8,128)S(1)} async-done(((f32[8,64,688]{2,1,0:T(8,128)}), f32[8,64,688]{2,1,0:T(8,128)S(1)}, u32[]{:S(2)}, u32[]{:S(2)}) %all-to-all-start) | async-done | bytes 1409056 | tf_op jit(solution)/shard_map/all_to_all | solution.py:14
  127.1 0.1 reduce_sum.9
  127.2 0.0 copy-done
  127.2 0.0 copy-done.1
  127.2 0.9 divide_convert_fusion
  128.0 0.9 broadcast_in_dim.2
  129.0 4.3 %all-to-all-start.1 = ((bf16[8,64,688]{2,1,0:T(8,128)(2,1)}), bf16[8,64,688]{2,1,0:T(8,128)(2,1)S(1)}, u32[]{:S(2)}, u32[]{:S(2)}) async-start(bf16[8,64,688]{2,1,0:T(8,128)(2,1)} %broadcast_in_dim.2), calls=%async_computation.1 | async-start | bytes 1572864 | tf_op jit(solution)/shard_map/all_to_all | solution.py:26
  133.3 12.3 %all-to-all-done.1 = bf16[8,64,688]{2,1,0:T(8,128)(2,1)S(1)} async-done(((bf16[8,64,688]{2,1,0:T(8,128)(2,1)}), bf16[8,64,688]{2,1,0:T(8,128)(2,1)S(1)}, u32[]{:S(2)}, u32[]{:S(2)}) %all-to-all-start.1) | async-done | bytes 704544 | tf_op jit(solution)/shard_map/all_to_all | solution.py:26
  145.6 2.5 %convolution_convert_fusion = bf16[512,688]{0,1:T(8,128)(2,1)} fusion(bf16[512,688]{1,0:T(8,128)(2,1)S(1)} %bitcast.9, bf16[4096,512]{1,0:T(8,128)(2,1)} %param.8, s32[]{:T(128)S(6)} %select_n.3), kind=kOutput, calls=%fused_computation | convolution fusion | flops 361062400 | bytes 1933316 | tf_op jit(solution)/shard_map/dot_general | solution.py:57
Async XLA Ops:
  7.2 80.6 %all-gather.2.cloned.1.call-start = ((), (), s32[]{:S(2)}) async-start(), calls=%async_computation.2 | async-start | bytes 8912896 | tf_op jit(solution)/shard_map/all_gather | solution.py:42
  101.1 26.0 %copy-start = (f32[64,688]{1,0:T(8,128)S(1)}, f32[64,688]{1,0:T(8,128)}, u32[]{:S(2)}) copy-start(f32[64,688]{1,0:T(8,128)} %param.10) | copy-start | bytes 528388
  101.1 26.1 %copy-start.1 = (f32[64,688]{1,0:T(8,128)S(1)}, f32[64,688]{1,0:T(8,128)}, u32[]{:S(2)}) copy-start(f32[64,688]{1,0:T(8,128)} %param.9) | copy-start | bytes 528388
  101.1 25.9 %all-to-all-start = ((f32[8,64,688]{2,1,0:T(8,128)}), f32[8,64,688]{2,1,0:T(8,128)S(1)}, u32[]{:S(2)}, u32[]{:S(2)}) async-start(f32[8,64,688]{2,1,0:T(8,128)} %bitcast), calls=%async_computation | async-start | bytes 3145728 | tf_op jit(solution)/shard_map/all_to_all | solution.py:14
  129.0 16.6 %all-to-all-start.1 = ((bf16[8,64,688]{2,1,0:T(8,128)(2,1)}), bf16[8,64,688]{2,1,0:T(8,128)(2,1)S(1)}, u32[]{:S(2)}, u32[]{:S(2)}) async-start(bf16[8,64,688]{2,1,0:T(8,128)(2,1)} %broadcast_in_dim.2), calls=%async_computation.1 | async-start | bytes 1572864 | tf_op jit(solution)/shard_map/all_to_all | solution.py:26
Sparse Core Ops, SparseCore 0:
  13.9 73.8 all-gather.1
where the time goes:
time: 155 us
  waiting for transfers between devices  106 us (68%)
  matrix products  22.4 us (14%)
  between operations  14.8 us (10%)
  starting transfers between devices  9.59 us (6%)
    all_gather x1, waiting for transfers between devices, per_device(): lax.all_gather(projected, 'tensor', axis=0, tiled=True)  74 us
    all_to_all x1, waiting for transfers between devices, sum_at_owner(): parts = lax.all_to_all(in_blocks(shard, dim, count), axis, 0, 0, tiled=True)  20 us
    dot_general x1, matrix products, per_device(): lax.dot_general(lax.all_gather(projected, 'tensor', axis=0, tiled=True),...  13.3 us
    all_to_all x1, waiting for transfers between devices, sent_to_all(): lax.all_to_all(jnp.broadcast_to(shard[None], (count, *shard.shape)), axis...  12.3 us
    dot_general x1, matrix products, per_device(): jnp.dot(activations, projection, preferred_element_type=jnp.float32)  6.59 us
    all_to_all x1, starting transfers between devices, sum_at_owner(): parts = lax.all_to_all(in_blocks(shard, dim, count), axis, 0, 0, tiled=True)  5.23 us
    all_to_all x1, starting transfers between devices, sent_to_all(): lax.all_to_all(jnp.broadcast_to(shard[None], (count, *shard.shape)), axis...  4.32 us
  transfers between devices with their start and end apart: 3, of which 3 were waited for; matrix products, arithmetic and copies ran while one was open for 0% of the time, Pallas kernels for 0%

commit v1 on v0

--- a/solution.py
+++ b/solution.py
@@ -1,7 +1,17 @@
+import functools
 import jax
 import jax.numpy as jnp
 from jax import lax
 from jax.sharding import PartitionSpec as P
+
+
+def _review_array(message, across):
+    return jnp.concatenate(
+        lax.all_to_all(jnp.stack(lax.axis_size(across) * [message], axis=0), across, 0, 0), axis=0
+    )
+
+
+_remake_chains = functools.partial(_review_array, across="tensor")
 
 
 def in_blocks(shard, dim, count):
@@ -39,7 +49,7 @@
     width = projection.shape[0]
     replica = lax.axis_index("dp")
     partial_grad = lax.dot_general(
-        lax.all_gather(projected, "tensor", axis=0, tiled=True),
+        _remake_chains(projected),
         cotangent,
         (((0,), (0,)), ((), ())),
         preferred_element_type=jnp.float32,

time: 155 us -> 197 us (1.27)
  blocking collectives: 0 us -> 102 us
  waiting for transfers between devices: 106 us -> 32.3 us
  local copies, waits for them, and re-layouts: 0.94 us -> 26.2 us
  between operations: 14.8 us -> 1.41 us
  starting transfers between devices: 9.59 us -> 11.8 us
    all_to_all x0 -> x1, blocking collectives: none -> 102 us  [_review_array(): lax.all_to_all(jnp.stack(lax.axis_size(across) * [message], axis=0), acro...]
    all_gather x1 -> x0, waiting for transfers between devices: 74 us -> none  [per_device(): lax.all_gather(projected, 'tensor', axis=0, tiled=True)]
    all_to_all x0 -> x1, local copies, waits for them, and re-layouts: none -> 12.3 us  [_review_array(): lax.all_to_all(jnp.stack(lax.axis_size(across) * [message], axis=0), acro...]
    dot_general x0 -> x1, local copies, waits for them, and re-layouts: none -> 11.9 us  [per_device(): lax.dot_general(_remake_chains(projected), cotangent, (((0,), (0,)), ((),...]
    all_to_all x1, starting transfers between devices: 5.23 us -> 7.44 us  [sum_at_owner(): parts = lax.all_to_all(in_blocks(shard, dim, count), axis, 0, 0, tiled=True)]
  transfers between devices with their start and end apart: 3 -> 2, of which waited for: 3 -> 2; matrix products, arithmetic and copies ran while one was open for 0% -> 0% of each run, Pallas kernels for 0% -> 0%
where the time goes in v1:
time: 197 us; the launch traced here: 196 us
  blocking collectives  102 us (52%)
  waiting for transfers between devices  32.3 us (16%)
  local copies, waits for them, and re-layouts  26.2 us (13%)
  matrix products  21.6 us (11%)
  starting transfers between devices  11.8 us (6%)
    all_to_all x1, blocking collectives, _review_array(): lax.all_to_all(jnp.stack(lax.axis_size(across) * [message], axis=0), acro...  102 us
    all_to_all x1, waiting for transfers between devices, sum_at_owner(): parts = lax.all_to_all(in_blocks(shard, dim, count), axis, 0, 0, tiled=True)  20 us
    dot_general x1, matrix products, per_device(): lax.dot_general(_remake_chains(projected), cotangent, (((0,), (0,)), ((),...  13.3 us
    all_to_all x1, local copies, waits for them, and re-layouts, _review_array(): lax.all_to_all(jnp.stack(lax.axis_size(across) * [message], axis=0), acro...  12.3 us
    all_to_all x1, waiting for transfers between devices, sent_to_all(): lax.all_to_all(jnp.broadcast_to(shard[None], (count, *shard.shape)), axis...  12.3 us
    dot_general x1, local copies, waits for them, and re-layouts, per_device(): lax.dot_general(_remake_chains(projected), cotangent, (((0,), (0,)), ((),...  11.9 us
    all_to_all x1, starting transfers between devices, sum_at_owner(): parts = lax.all_to_all(in_blocks(shard, dim, count), axis, 0, 0, tiled=True)  7.44 us
    dot_general x1, matrix products, per_device(): jnp.dot(activations, projection, preferred_element_type=jnp.float32)  5.79 us
  transfers between devices with their start and end apart: 2, of which 2 were waited for; matrix products, arithmetic and copies ran while one was open for 0% of the time, Pallas kernels for 0%

profile of v1, /device:TPU:1, one launch (start us, length us, event | category | flops | bytes accessed | tf_op | source)
XLA Modules:
  0.0 196.5 jit_solution(14682324265484842137)
XLA Ops:
  0.6 5.8 %convolution_convert_fusion.1 = bf16[512,512]{1,0:T(8,128)(2,1)S(1)} fusion(bf16[512,4096]{1,0:T(8,128)(2,1)} %param.6, bf16[4096,512]{1,0:T(8,128)(2,1)} %param.8), kind=kOutput, calls=%fused_computation.3 | convolution fusion | flops 2147745792 | bytes 8912896 | tf_op jit(solution)/shard_map/dot_general | solution.py:46
  6.4 0.2 copy.11
  6.6 0.8 stack.2
  7.5 102.3 %all_to_all.15 = bf16[16,512,512]{1,2,0:T(8,128)(2,1)} all-to-all(bf16[16,512,512]{1,2,0:T(8,128)(2,1)S(1)} %stack.2), channel_id=1, replica_groups=mesh['dp'=8,'tensor'=16] {'tensor'}, dimensions={0} | all-to-all | bytes 16777216 | tf_op jit(solution)/shard_map/all_to_all | solution.py:10
  109.7 12.3 %copy.12 = bf16[16,512,512]{2,1,0:T(8,128)(2,1)} copy(bf16[16,512,512]{1,2,0:T(8,128)(2,1)} %all_to_all.15) | data formatting | bytes 16777216 | tf_op jit(solution)/shard_map/all_to_all | solution.py:10
  122.1 11.9 %copy.13 = bf16[512,8192]{1,0:T(8,128)(2,1)} copy(bf16[512,8192]{0,1:T(8,128)(2,1)} %bitcast.14) | data formatting | bytes 16777216 | tf_op jit(solution)/shard_map/dot_general | solution.py:51
  134.0 13.3 %fusion = f32[8,64,688]{2,1,0:T(8,128)} fusion(bf16[8,64,8192]{2,1,0:T(8,128)(2,1)} %bitcast.15, bf16[8192,688]{0,1:T(8,128)(2,1)} %param.7), kind=kOutput, calls=%fused_computation | convolution fusion | flops 5771362304 | bytes 21069824 | tf_op jit(solution)/shard_map/dot_general | solution.py:51
  147.3 0.0 copy-start
  147.3 0.0 copy-start.1
  147.3 7.4 %all-to-all-start.1 = ((f32[8,64,688]{2,1,0:T(8,128)}), f32[8,64,688]{2,1,0:T(8,128)S(1)}, u32[]{:S(2)}, u32[]{:S(2)}) async-start(f32[8,64,688]{2,1,0:T(8,128)} %fusion), calls=%async_computation.1 | async-start | bytes 3145728 | tf_op jit(solution)/shard_map/all_to_all | solution.py:24
  155.4 20.0 %all-to-all-done.1 = f32[8,64,688]{2,1,0:T(8,128)S(1)} async-done(((f32[8,64,688]{2,1,0:T(8,128)}), f32[8,64,688]{2,1,0:T(8,128)S(1)}, u32[]{:S(2)}, u32[]{:S(2)}) %all-to-all-start.1) | async-done | bytes 1409056 | tf_op jit(solution)/shard_map/all_to_all | solution.py:24
  175.4 0.1 reduce_sum.9
  175.5 0.0 copy-done
  175.5 0.0 copy-done.1
  175.5 0.9 divide_convert_fusion
  176.4 0.9 broadcast_in_dim.2
  177.4 4.3 %all-to-all-start.2 = ((bf16[8,64,688]{2,1,0:T(8,128)(2,1)}), bf16[8,64,688]{2,1,0:T(8,128)(2,1)S(1)}, u32[]{:S(2)}, u32[]{:S(2)}) async-start(bf16[8,64,688]{2,1,0:T(8,128)(2,1)} %broadcast_in_dim.2), calls=%async_computation.2 | async-start | bytes 1572864 | tf_op jit(solution)/shard_map/all_to_all | solution.py:36
  181.7 12.3 %all-to-all-done.2 = bf16[8,64,688]{2,1,0:T(8,128)(2,1)S(1)} async-done(((bf16[8,64,688]{2,1,0:T(8,128)(2,1)}), bf16[8,64,688]{2,1,0:T(8,128)(2,1)S(1)}, u32[]{:S(2)}, u32[]{:S(2)}) %all-to-all-start.2) | async-done | bytes 704544 | tf_op jit(solution)/shard_map/all_to_all | solution.py:36
  194.0 2.5 %convolution_convert_fusion = bf16[512,688]{0,1:T(8,128)(2,1)} fusion(bf16[512,688]{1,0:T(8,128)(2,1)S(1)} %bitcast.16, bf16[4096,512]{1,0:T(8,128)(2,1)} %param.8, s32[]{:T(128)S(6)} %select_n.3), kind=kOutput, calls=%fused_computation.2 | convolution fusion | flops 361062400 | bytes 1933316 | tf_op jit(solution)/shard_map/dot_general | solution.py:67
Async XLA Ops:
  147.3 28.3 %copy-start = (f32[64,688]{1,0:T(8,128)S(1)}, f32[64,688]{1,0:T(8,128)}, u32[]{:S(2)}) copy-start(f32[64,688]{1,0:T(8,128)} %param.10) | copy-start | bytes 528388
  147.3 28.3 %copy-start.1 = (f32[64,688]{1,0:T(8,128)S(1)}, f32[64,688]{1,0:T(8,128)}, u32[]{:S(2)}) copy-start(f32[64,688]{1,0:T(8,128)} %param.9) | copy-start | bytes 528388
  147.3 28.2 %all-to-all-start.1 = ((f32[8,64,688]{2,1,0:T(8,128)}), f32[8,64,688]{2,1,0:T(8,128)S(1)}, u32[]{:S(2)}, u32[]{:S(2)}) async-start(f32[8,64,688]{2,1,0:T(8,128)} %fusion), calls=%async_computation.1 | async-start | bytes 3145728 | tf_op jit(solution)/shard_map/all_to_all | solution.py:24
  177.4 16.6 %all-to-all-start.2 = ((bf16[8,64,688]{2,1,0:T(8,128)(2,1)}), bf16[8,64,688]{2,1,0:T(8,128)(2,1)S(1)}, u32[]{:S(2)}, u32[]{:S(2)}) async-start(bf16[8,64,688]{2,1,0:T(8,128)(2,1)} %broadcast_in_dim.2), calls=%async_computation.2 | async-start | bytes 1572864 | tf_op jit(solution)/shard_map/all_to_all | solution.py:36
